TPU v7x, 256 devices: a whole 4x4x8 slice. The times are simulated.
256 devices in a mesh: dp: 2 (over core), cp: 16 (over y_hi, z), tp: 8 (over x, y_lo).
Axes of the slice: x: 4, y: 4 (y_hi: 2, y_lo: 2; y = y_hi * 2 + y_lo), z: 8, core: 2. Of those that a mesh axis runs over, the one named last changes fastest.
Arguments:
- queries: bfloat16 [2, 8192, 64, 128], P('dp', 'cp', 'tp'), may hold values from -5 to 5
- keys: bfloat16 [2, 8192, 8, 128], P('dp', 'cp', 'tp'), may hold values from -5 to 5
- values: bfloat16 [2, 8192, 8, 128], P('dp', 'cp', 'tp'), may hold values from -6 to 6
- output_gradient: bfloat16 [2, 8192, 64, 128], P('dp', 'cp', 'tp'), may hold values from -48 to 48
- lengths: int32 [2, 12], P('dp'), may hold values from 1 to 1024, 8192 in all within a row
Outputs:
- query_grad: bfloat16 [2, 8192, 64, 128], P('dp', 'cp', 'tp')
- key_grad: bfloat16 [2, 8192, 8, 128], P('dp', 'cp', 'tp')
- value_grad: bfloat16 [2, 8192, 8, 128], P('dp', 'cp', 'tp')
- q_bias_grad: float32 [64, 128], P('tp')
Inputs may be any that keep to these rules, and one draw needn't show every extreme that they name: Each row holds the lengths of one pack's 12 responses in pack order; they sum to 8192, and the longest is exactly 1024 tokens.
All inputs are finite; a program needn't handle non-finite values.
Results may differ from a plain program's by a relative error of at most 0.0077.
Values may be sent and summed in bfloat16 or wider, within the bound.
No kernel may reach another device: no remote copies, remote signals or barrier semaphores. Data moves between devices by JAX's collectives and lax.ppermute only.
A program may use at most 64 MiB of HBM per device.

v0:
```python
import functools
import math

import jax
import jax.numpy as jnp
from jax import lax
from jax.experimental import pallas as pl
from jax.experimental.pallas import tpu as pltpu
from jax.sharding import PartitionSpec as P

NEGATIVE = -1e30
LOG2E = math.log2(math.e)

NT = (((1,), (1,)), ((), ()))
NN = (((1,), (0,)), ((), ()))

ROWS = 2048
CHUNK = 256
FAR_CHUNK = 128
VMEM_LIMIT = 20 << 20
MOST_ITEMS = 32
FAR_SLOTS = 4


def dot(a, b, dims):
    return lax.dot_general(a, b, dims, preferred_element_type=jnp.float32)


def block_index():
    return lax.axis_index("cp")


def doc_ends(len_ref, tokens):
    end = -block_index() * tokens
    ends = [end]
    for j in range(len_ref.shape[1]):
        end = end + len_ref[0, j]
        ends.append(end)
    return ends


def low_of(ends, pos):
    low = ends[0]
    for end in ends[1:]:
        low = jnp.where(end <= pos, end, low)
    return low


def plan(len_ref, tokens, rows, group, origin, chunk, items_ref):
    ends = doc_ends(len_ref, tokens)
    span = ROWS // group
    count = jnp.int32(0)
    for j in range(rows // ROWS):
        items_ref[MOST_ITEMS + j] = count
        t0, t1 = j * span, (j + 1) * span - 1
        low0, low1 = low_of(ends, jnp.int32(t0)), low_of(ends, jnp.int32(t1))
        begin = jnp.maximum(low0 - origin, 0) // chunk
        end = min((t1 - origin) // chunk + 1, tokens // chunk)

        def put(c, count):
            start = c * chunk + origin
            masked = (low1 > start) | (start + chunk - 1 > t0)
            items_ref[count] = j * 64 + c * 2 + masked.astype(jnp.int32)
            return count + 1

        count = lax.fori_loop(begin, end, put, count)
    return count


def each_item(items_ref, begin, end, chunk, step):
    @pl.loop(begin, end)
    def _(i):
        item = items_ref[i]
        tile = item // 64
        first = pl.multiple_of((item // 2) % 32 * chunk, chunk)

        @pl.when(item % 2 == 1)
        def _():
            step(i, tile, first, True)

        @pl.when(item % 2 == 0)
        def _():
            step(i, tile, first, False)


def each_kept(items_ref, begin, end, chunk, step):
    @pl.loop(begin, end)
    def _(i):
        item = items_ref[i]
        step(i, item // 64, pl.multiple_of((item // 2) % 32 * chunk, chunk))


def each_near(len_ref, tokens, tile, group, whole, half):
    ends = doc_ends(len_ref, tokens)
    span = ROWS // group
    low0, low1 = low_of(ends, tile * span), low_of(ends, (tile + 1) * span - 1)
    for masked in (True, False):

        @pl.when((low0 < CHUNK - tokens) & ((low1 > -tokens) == masked))
        def _():
            whole(masked)

    @pl.when((low0 >= CHUNK - tokens) & (low0 < 0))
    def _():
        half()


def tile_rows(tile):
    return pl.ds(pl.multiple_of(tile * ROWS, ROWS), ROWS)


def early_slot(i, tile, first, chunk):
    return pl.ds(0, chunk)


def own_slot(i, tile, first, chunk):
    return pl.ds(pl.multiple_of((tile * (tile + 1) // 2 - 1) * CHUNK + first, CHUNK), chunk)


def near_slot(i, tile, first, chunk):
    return pl.ds(pl.multiple_of(tile * 2 * CHUNK + first, CHUNK), chunk)


def far_slot(i, tile, first, chunk):
    return pl.ds(pl.multiple_of(i * FAR_CHUNK, FAR_CHUNK), chunk)


def hide(x, start, rows, see_ref):
    low = see_ref[0:1, rows] - start
    key = lax.broadcasted_iota(jnp.int32, x.shape, 0)
    seen = (key - low).astype(jnp.uint32) <= see_ref[1:2, rows].astype(jnp.uint32)
    return jnp.where(seen, x, NEGATIVE)


def add_stats(scale2, origin, chunk, q_ref, g_ref, k_ref, v_ref, see_ref, st_ref, s_ref, dp_ref, slot_of, i, tile, first, masked):
    rows, keys, slot = tile_rows(tile), pl.ds(first, chunk), slot_of(i, tile, first, chunk)
    scores = dot(k_ref[keys, :], q_ref[rows, :], NT) * scale2
    dprob = dot(v_ref[keys, :], g_ref[rows, :], NT)
    if masked:
        scores = hide(scores, first + origin, rows, see_ref)
    s_ref[slot, :] = scores
    dp_ref[slot, :] = dprob
    top_old = st_ref[0:1, rows]
    top = jnp.maximum(top_old, jnp.max(scores, axis=0, keepdims=True))
    expo = jnp.exp2(scores - top)
    factor = jnp.exp2(top_old - top)
    st_ref[0:1, rows] = top
    st_ref[1:2, rows] = st_ref[1:2, rows] * factor + jnp.sum(expo, axis=0, keepdims=True)
    st_ref[2:3, rows] = st_ref[2:3, rows] * factor + jnp.sum(expo * dprob, axis=0, keepdims=True)


def add_grads(chunk, q_ref, g_ref, kt_ref, st_ref, dqt_ref, sum_ref, s_ref, dp_ref, slot_of, i, tile, first):
    head = q_ref.shape[1]
    rows, keys, slot = tile_rows(tile), pl.ds(first, chunk), slot_of(i, tile, first, chunk)
    prob = jnp.exp2(s_ref[slot, :] - st_ref[0:1, rows])
    dscore = (prob * (dp_ref[slot, :] - st_ref[1:2, rows])).astype(jnp.bfloat16)
    sum_ref[keys, 0:head] += dot(dscore, q_ref[rows, :], NN)
    sum_ref[keys, head:] += dot(prob.astype(jnp.bfloat16), g_ref[rows, :], NN)
    dqt_ref[:, rows] += dot(kt_ref[:, keys], dscore, NN)


def early_stats(group, scale2, len_ref, q_hbm, g_hbm, k_hbm, v_hbm, q_ref, g_ref, k_ref, v_ref, see_ref, st_ref, s_ref, dp_ref,
                items_ref, sems):
    tokens = k_ref.shape[0]
    count_rows = q_ref.shape[0]
    fetches = [
        pltpu.make_async_copy(source, target, sems.at[n])
        for n, (source, target) in enumerate((
            (k_hbm, k_ref),
            (q_hbm.at[0:ROWS, :], q_ref.at[0:ROWS, :]),
            (v_hbm, v_ref),
            (g_hbm.at[0:ROWS, :], g_ref.at[0:ROWS, :]),
            (q_hbm.at[ROWS:, :], q_ref.at[ROWS:, :]),
            (g_hbm.at[ROWS:, :], g_ref.at[ROWS:, :]),
        ))
    ]
    for fetch in fetches:
        fetch.start()
    pos = lax.broadcasted_iota(jnp.int32, (1, count_rows), 1) // group
    low = low_of(doc_ends(len_ref, tokens), pos)
    see_ref[0:1, :] = low
    see_ref[1:2, :] = pos - low
    st_ref[0:1, :] = jnp.full((1, count_rows), NEGATIVE, jnp.float32)
    st_ref[1:3, :] = jnp.zeros((2, count_rows), jnp.float32)
    for fetch in fetches[:4]:
        fetch.wait()
    add_stats(scale2, 0, CHUNK, q_ref, g_ref, k_ref, v_ref, see_ref, st_ref, s_ref, dp_ref, early_slot, 0, 0, 0, True)
    for fetch in fetches[4:]:
        fetch.wait()


def near_stats(group, scale2, len_ref, q_ref, g_ref, k0_ref, v0_ref, k1_ref, v1_ref, see_ref, st_in,
               st_ref, s0_ref, dp0_ref, s1_ref, dp1_ref, kt0_ref, kt1_ref, items_ref):
    tokens = k0_ref.shape[0]
    st_ref[...] = st_in[...]
    kt0_ref[...] = k0_ref[...].T
    kt1_ref[...] = k1_ref[...].T
    count = plan(len_ref, tokens, q_ref.shape[0], group, 0, CHUNK, items_ref)
    each_item(items_ref, items_ref[MOST_ITEMS + 1], count, CHUNK, functools.partial(
        add_stats, scale2, 0, CHUNK, q_ref, g_ref, k0_ref, v0_ref, see_ref, st_ref, s0_ref, dp0_ref, own_slot))

    @pl.loop(0, q_ref.shape[0] // ROWS)
    def _(j):
        def add(chunk, first, masked):
            add_stats(scale2, -tokens, chunk, q_ref, g_ref, k1_ref, v1_ref, see_ref, st_ref, s1_ref, dp1_ref, near_slot,
                      0, j, first, masked)

        each_near(len_ref, tokens, j, group,
                  lambda masked: add(tokens, 0, masked), lambda: add(CHUNK, tokens - CHUNK, True))


def far_grads(group, scale2, len_ref, q_ref, g_ref, kv_ref, see_ref, st_in,
              st_ref, far_ref, dqt_ref, run_ref, sum_ref, kt_ref, s_ref, dp_ref, items_ref):
    tokens = kv_ref.shape[0]
    head = q_ref.shape[1]
    k_ref, v_ref = kv_ref.at[:, 0:head], kv_ref.at[:, head:]
    origin = -2 * tokens
    run_ref[...] = st_in[...]
    dqt_ref[...] = jnp.zeros_like(dqt_ref)
    sum_ref[...] = jnp.zeros_like(sum_ref)
    kt_ref[...] = k_ref[...].T
    count = plan(len_ref, tokens, q_ref.shape[0], group, origin, FAR_CHUNK, items_ref)
    each_item(items_ref, 0, count, FAR_CHUNK, functools.partial(
        add_stats, scale2, origin, FAR_CHUNK, q_ref, g_ref, k_ref, v_ref, see_ref, run_ref, s_ref, dp_ref, far_slot))
    total = run_ref[1:2, :]
    st_ref[0:1, :] = run_ref[0:1, :] + jnp.log2(total)
    st_ref[1:2, :] = run_ref[2:3, :] / total
    each_kept(items_ref, 0, count, FAR_CHUNK, functools.partial(
        add_grads, FAR_CHUNK, q_ref, g_ref, kt_ref, st_ref, dqt_ref, sum_ref, s_ref, dp_ref, far_slot))
    far_ref[...] = sum_ref[...].astype(far_ref.dtype)


def main_grads(group, scale, len_ref, q_ref, g_ref, kt1_ref, kt0_ref, s1_ref, dp1_ref, se_ref, dpe_ref, s0_ref, dp0_ref,
               st_ref, dqt_ref, dq_hbm, near_ref, own_ref, bias_ref, unused, dq_ref, items0_ref, sems):
    count_rows, head = q_ref.shape
    tokens = kt0_ref.shape[1]
    tiles = count_rows // ROWS
    near_ref[...] = jnp.zeros_like(near_ref)
    own_ref[...] = jnp.zeros_like(own_ref)
    bias_ref[...] = jnp.zeros_like(bias_ref)
    items0_ref[MOST_ITEMS + tiles] = plan(len_ref, tokens, count_rows, group, 0, CHUNK, items0_ref)

    def copy(j):
        return pltpu.make_async_copy(dq_ref.at[tile_rows(j), :], dq_hbm.at[tile_rows(j), :], sems.at[j])

    @pl.loop(0, tiles)
    def _(j):
        low0 = low_of(doc_ends(len_ref, tokens), j * (ROWS // group))
        for chunk, live in ((tokens, low0 < CHUNK - tokens), (CHUNK, (low0 >= CHUNK - tokens) & (low0 < 0))):

            @pl.when(live)
            def _():
                add_grads(chunk, q_ref, g_ref, kt1_ref, st_ref, dqt_ref, near_ref, s1_ref, dp1_ref, near_slot,
                          0, j, tokens - chunk)

        @pl.when(j == 0)
        def _():
            add_grads(CHUNK, q_ref, g_ref, kt0_ref, st_ref, dqt_ref, own_ref, se_ref, dpe_ref, early_slot, 0, 0, 0)

        @pl.when(j > 0)
        def _():
            each_kept(items0_ref, items0_ref[MOST_ITEMS + j], items0_ref[MOST_ITEMS + j + 1], CHUNK, functools.partial(
                add_grads, CHUNK, q_ref, g_ref, kt0_ref, st_ref, dqt_ref, own_ref, s0_ref, dp0_ref, own_slot))

        rows = tile_rows(j)
        dq = (dqt_ref[:, rows] * scale).astype(dq_ref.dtype).T
        dq_ref[rows, :] = dq
        copy(j).start()
        bias_ref[...] += jnp.sum(dq.astype(jnp.float32).reshape(ROWS // group, group, head), axis=0)

    for j in range(tiles):
        copy(j).wait()


def combine(scale, root, own_ref, near_ref, bias_ref, dk_ref, dv_ref, db_ref):
    head = dk_ref.shape[1]
    total = own_ref[...] + near_ref[...].astype(jnp.float32)
    dk_ref[...] = (scale * total[:, :head]).astype(dk_ref.dtype)
    dv_ref[...] = total[:, head:].astype(dv_ref.dtype)
    db_ref[...] = jnp.sum(bias_ref[...].astype(jnp.float32), axis=0) / root


SMEM = pl.BlockSpec(memory_space=pltpu.SMEM)
VMEM = pl.BlockSpec(memory_space=pltpu.VMEM)
HBM = pl.BlockSpec(memory_space=pltpu.HBM)


def call(kernel, specs, args, outs, scratch, flops, out_specs=None, aliases={}):
    return pl.pallas_call(
        kernel,
        out_shape=outs,
        in_specs=specs,
        out_specs=out_specs or jax.tree.map(lambda _: VMEM, outs),
        input_output_aliases=aliases,
        scratch_shapes=scratch,
        compiler_params=pltpu.CompilerParams(vmem_limit_bytes=VMEM_LIMIT),
        cost_estimate=pl.CostEstimate(flops=flops, bytes_accessed=4 << 20, transcendentals=0),
    )(*args)


ITEMS = pltpu.SMEM((MOST_ITEMS + 16,), jnp.int32)


def array(dtype, *shape):
    return jax.ShapeDtypeStruct(shape, dtype)


def early_part(lengths, q_hbm, g_hbm, k_hbm, v_hbm, heads):
    rows, head = q_hbm.shape
    bf16, f32 = jnp.bfloat16, jnp.float32
    return call(
        functools.partial(early_stats, heads, LOG2E / math.sqrt(head)),
        [SMEM] + [HBM] * 4,
        (lengths, q_hbm, g_hbm, k_hbm, v_hbm),
        (array(bf16, rows, head), array(bf16, rows, head), array(bf16, *k_hbm.shape), array(bf16, *k_hbm.shape),
         array(jnp.int32, 2, rows), array(f32, 3, rows), array(f32, CHUNK, ROWS), array(f32, CHUNK, ROWS)),
        [ITEMS, pltpu.SemaphoreType.DMA((6,))],
        rows * k_hbm.size * 2,
    )


def near_part(lengths, q, g, k0, v0, k1, v1, see, st, heads):
    rows, head = q.shape
    tokens = k0.shape[0]
    tiles = rows // ROWS
    own = array(jnp.float32, (tiles * (tiles + 1) // 2 - 1) * CHUNK, ROWS)
    near = array(jnp.float32, tiles * tokens, ROWS)
    return call(
        functools.partial(near_stats, heads, LOG2E / math.sqrt(head)),
        [SMEM] + [VMEM] * 8,
        (lengths, q, g, k0, v0, k1, v1, see, st),
        (array(jnp.float32, 3, rows), own, own, near, near, array(k0.dtype, head, tokens), array(k0.dtype, head, tokens)),
        [ITEMS],
        rows * k0.size * 6,
    )


def far_part(lengths, q, g, kv2, see, st, heads):
    rows, head = q.shape
    tokens = kv2.shape[0]
    bf16, f32 = jnp.bfloat16, jnp.float32
    return call(
        functools.partial(far_grads, heads, LOG2E / math.sqrt(head)),
        [SMEM] + [VMEM] * 5,
        (lengths, q, g, kv2, see, st),
        (array(f32, 2, rows), array(bf16, tokens, 2 * head), array(f32, head, rows)),
        [pltpu.VMEM((3, rows), f32), pltpu.VMEM((tokens, 2 * head), f32), pltpu.VMEM((head, tokens), bf16),
         *(pltpu.VMEM((FAR_SLOTS * FAR_CHUNK, ROWS), f32),) * 2, ITEMS],
        rows * kv2.size,
    )


def main_part(lengths, q, g, kt1, kt0, kept, st, dqt, heads):
    rows, head = q.shape
    tokens = kt0.shape[1]
    bf16, f32 = jnp.bfloat16, jnp.float32
    return call(
        functools.partial(main_grads, heads, 1.0 / math.sqrt(head)),
        [SMEM] + [VMEM] * 12,
        (lengths, q, g, kt1, kt0, *kept, st, dqt),
        (array(bf16, rows, head), array(f32, tokens, 2 * head), array(f32, tokens, 2 * head), array(f32, heads, head),
         array(f32, *dqt.shape)),
        [pltpu.VMEM((rows, head), bf16), ITEMS, pltpu.SemaphoreType.DMA((rows // ROWS,))],
        rows * tokens * head * 12,
        out_specs=(HBM, VMEM, VMEM, VMEM, VMEM),
        aliases={12: 4},
    )[:4]


def body(queries, keys, values, output_gradient, lengths):
    tokens, heads, head = queries.shape[1:]
    rows = tokens * heads
    cp = lax.axis_size("cp")
    bf16, f32 = jnp.bfloat16, jnp.float32
    q_hbm, g_hbm, k_hbm, v_hbm = (
        pltpu.with_memory_space_constraint(x.reshape(-1, head), pltpu.HBM)
        for x in (queries, output_gradient, keys, values)
    )

    def shift(x, steps):
        return lax.ppermute(x, "cp", [(i, i + steps) for i in range(max(0, -steps), min(cp, cp - steps))])

    k1, v1 = shift(keys.reshape(tokens, head), 1), shift(values.reshape(tokens, head), 1)
    q, g, k0, v0, see, st, *early = early_part(lengths, q_hbm, g_hbm, k_hbm, v_hbm, heads)
    k1, v1, st = lax.optimization_barrier((k1, v1, st))
    kv2 = shift(jnp.concatenate([k1, v1], axis=1), 1)
    st, s0, dp0, s1, dp1, kt0, kt1 = near_part(lengths, q, g, k0, v0, k1, v1, see, st, heads)
    st, far, dqt = far_part(lengths, q, g, kv2, see, st, heads)
    far = shift(far, -1)
    dq, near, own, bias = main_part(lengths, q, g, kt1, kt0, (s1, dp1, *early, s0, dp0), st, dqt, heads)
    dp = lax.axis_size("dp")
    near, bias = lax.optimization_barrier(((near + far.astype(f32)).astype(bf16), bias))
    near = shift(near, -1)
    bias += sum(lax.ppermute(bias, "dp", [(i, (i + n) % dp) for i in range(dp)]) for n in range(1, dp))
    bias = lax.all_to_all(jnp.broadcast_to(bias.astype(bf16), (cp, heads, head)), "cp", 0, 0)
    root = math.sqrt(dp * cp * tokens)
    key_grad, value_grad, q_bias_grad = call(
        functools.partial(combine, 1.0 / math.sqrt(head), root),
        [VMEM] * 3,
        (own, near, bias),
        (array(bf16, tokens, head), array(bf16, tokens, head), array(f32, heads, head)),
        [],
        1000,
    )
    return (
        dq.reshape(queries.shape),
        key_grad.reshape(keys.shape),
        value_grad.reshape(values.shape),
        q_bias_grad,
    )


def solution(mesh):
    placed = (
        P("dp", "cp", "tp", None),
        P("dp", "cp", "tp", None),
        P("dp", "cp", "tp", None),
        P("dp", "cp", "tp", None),
        P("dp", None),
    )
    return jax.shard_map(
        body,
        mesh=mesh,
        in_specs=placed,
        out_specs=(
            P("dp", "cp", "tp", None),
            P("dp", "cp", "tp", None),
            P("dp", "cp", "tp", None),
            P("tp", None),
        ),
        check_vma=False,
    )
```

profile of v0, /device:TPU:2, one launch (start us, length us, event | category | flops | bytes accessed | tf_op | source)
XLA Modules:
  0.0 63.2 jit_solution(10084743064258627786)
XLA Ops:
  0.6 3.8 %collective-permute-start = (bf16[512,128]{1,0:T(8,128)(2,1)}, bf16[512,128]{1,0:T(8,128)(2,1)S(1)}, u32[]{:S(2)}, u32[]{:S(2)}) collective-permute-start(bf16[512,128]{1,0:T(8,128)(2,1)} %bitcast.9), channel_id=1, source_target_pairs={{0,8},{8,16},{16,24},{24,32},{32,40},{40,48},{48,56},{56,64},{64,7... | collective-permute-start | bytes 393224 | tf_op jit(solution)/shard_map/ppermute | solution.py:381
  4.5 3.8 %collective-permute-start.1 = (bf16[512,128]{1,0:T(8,128)(2,1)}, bf16[512,128]{1,0:T(8,128)(2,1)S(1)}, u32[]{:S(2)}, u32[]{:S(2)}) collective-permute-start(bf16[512,128]{1,0:T(8,128)(2,1)} %bitcast.11), channel_id=1, source_target_pairs={{0,8},{8,16},{16,24},{24,32},{32,40},{40,48},{48,56},{56,64},{64,7... | collective-permute-start | bytes 393224 | tf_op jit(solution)/shard_map/ppermute | solution.py:381
  8.3 0.0 copy-start
  8.3 0.6 %copy-done = s32[1,12]{1,0:T(1,128)S(1)} copy-done((s32[1,12]{1,0:T(1,128)S(1)}, s32[1,12]{1,0:T(1,128)}, u32[]{:S(2)}) %copy-start) | copy-done | bytes 72
  9.0 2.9 %shard_map.84 = (bf16[4096,128]{1,0:T(8,128)(2,1)S(1)}, bf16[4096,128]{1,0:T(8,128)(2,1)S(1)}, bf16[512,128]{1,0:T(8,128)(2,1)S(1)}, bf16[512,128]{1,0:T(8,128)(...) custom-call(s32[1,12]{1,0:T(1,128)S(1)} %copy-done, ...), custom_call_target="tpu_custom_call" | custom-call | flops 536870912 | bytes 4194304 | tf_op jit(solution)/shard_map/pallas_call | solution.py:289
  11.9 0.0 collective-permute-done.k1_ref
  11.9 0.0 collective-permute-done.1.v1_ref
  12.0 3.8 %collective-permute-start.2 = (bf16[512,256]{1,0:T(8,128)(2,1)S(1)}, bf16[512,256]{1,0:T(8,128)(2,1)S(1)}, u32[]{:S(2)}, u32[]{:S(2)}) collective-permute-start(bf16[512,256]{1,0:T(8,128)(2,1)S(1)} %pad_maximum_fusion), channel_id=1, source_target_pairs={{0,8},{8,16},{16,24},{24,32},{32,40},{40,48},{48,56},{56,64},{64,7... | collective-permute-start | bytes 786440 | tf_op jit(solution)/shard_map/ppermute | solution.py:381
  15.8 2.7 %shard_map.85 = (f32[3,4096]{1,0:T(4,128)S(1)}, f32[512,2048]{1,0:T(8,128)S(1)}, f32[512,2048]{1,0:T(8,128)S(1)}, f32[1024,2048]{1,0:T(8,128)S(1)}, f32[1024,204...) custom-call(s32[1,12]{1,0:T(1,128)S(1)} %copy-done, ...), custom_call_target="tpu_custom_call" | custom-call | flops 1610612736 | bytes 4194304 | tf_op jit(solution)/shard_map/pallas_call | solution.py:289
  18.5 2.2 %collective-permute-done.2.kv_ref = bf16[512,256]{1,0:T(8,128)(2,1)S(1)} collective-permute-done((bf16[512,256]{1,0:T(8,128)(2,1)S(1)}, bf16[512,256]{1,0:T(8,128)(2,1)S(1)}, u32[]{:S(2)}, u32[]{:S(2)}) %collective-permute-start.2) | collective-permute-done | bytes 262176 | tf_op jit(solution)/shard_map/ppermute | solution.py:381
  20.8 0.8 %shard_map.86 = (f32[2,4096]{1,0:T(2,128)S(1)}, bf16[512,256]{1,0:T(8,128)(2,1)S(1)}, f32[128,4096]{1,0:T(8,128)S(1)}) custom-call(s32[1,12]{1,0:T(1,128)S(1)} %copy-done, bf16[4096,128]{1,0:T(8,128)(2,1)S(1)} %get-tuple-element.34.q_ref, bf16[4096,128]{1,0:T(8,128)(2,1)S(1)} %get-tuple-element.35.g_ref, bf16[512,256]{1,0:T(8,128)(2,1)S(1)} %collective-permute-done.2.kv_ref, ...), custom_call_target="tpu_custom_call" | custom-call | flops 536870912 | bytes 4194304 | tf_op jit(solution)/shard_map/pallas_call | solution.py:289
  21.6 1.3 %collective-permute-start.3 = (bf16[512,256]{1,0:T(8,128)(2,1)S(1)}, bf16[512,256]{1,0:T(8,128)(2,1)S(1)}, u32[]{:S(2)}, u32[]{:S(2)}) collective-permute-start(bf16[512,256]{1,0:T(8,128)(2,1)S(1)} %get-tuple-element.57), channel_id=1, source_target_pairs={{8,0},{16,8},{24,16},{32,24},{40,32},{48,40},{56,48},{64,56},{72,6... | collective-permute-start | bytes 786440 | tf_op jit(solution)/shard_map/ppermute | solution.py:381
  22.9 5.3 %shard_map.87 = (bf16[4096,128]{1,0:T(8,128)(2,1)}, f32[512,256]{1,0:T(8,128)S(1)}, f32[512,256]{1,0:T(8,128)S(1)}, f32[8,128]{1,0:T(8,128)S(1)}, f32[128,4096]{1,0:T(8,128)S(1)}) custom-call(s32[1,12]{1,0:T(1,128)S(1)} %copy-done, bf16[4096,128]{1,0:T(8,128)(2,1)S(1)} %get-tuple-element.34.q_ref, ...), custom_call_target="tpu_custom_call", output_to_operand_aliasing={{4}: (12, {})} | custom-call | flops 3221225472 | bytes 4194304 | tf_op jit(solution)/shard_map/pallas_call | solution.py:289
  28.1 4.8 %collective-permute-done.3 = bf16[512,256]{1,0:T(8,128)(2,1)S(1)} collective-permute-done((bf16[512,256]{1,0:T(8,128)(2,1)S(1)}, bf16[512,256]{1,0:T(8,128)(2,1)S(1)}, u32[]{:S(2)}, u32[]{:S(2)}) %collective-permute-start.3) | collective-permute-done | bytes 262176 | tf_op jit(solution)/shard_map/ppermute | solution.py:381
  32.9 0.1 add_convert_fusion
  33.0 0.1 collective-permute-start.5
  33.1 1.3 %collective-permute-start.4 = (bf16[512,256]{1,0:T(8,128)(2,1)S(1)}, bf16[512,256]{1,0:T(8,128)(2,1)S(1)}, u32[]{:S(2)}, u32[]{:S(2)}) collective-permute-start(bf16[512,256]{1,0:T(8,128)(2,1)S(1)} %add_convert_fusion), channel_id=1, source_target_pairs={{8,0},{16,8},{24,16},{32,24},{40,32},{48,40},{56,48},{64,56},{72,6... | collective-permute-start | bytes 786440 | tf_op jit(solution)/shard_map/ppermute | solution.py:381
  34.4 0.0 collective-permute-done.5
  34.4 28.0 %all_to_all.5.bias_ref = bf16[16,8,128]{2,1,0:T(8,128)(2,1)S(1)} all-to-all(bf16[16,8,128]{2,1,0:T(8,128)(2,1)S(1)} %broadcast_in_dim.3), channel_id=1, replica_groups=mesh['dp'=2,'cp'=16,'tp'=8] {'cp'}, dimensions={0} | all-to-all | bytes 65536 | tf_op jit(solution)/shard_map/all_to_all | solution.py:395
  62.4 0.0 collective-permute-done.4.near_ref
  62.4 0.8 %shard_map.88 = (bf16[512,128]{1,0:T(8,128)(2,1)}, bf16[512,128]{1,0:T(8,128)(2,1)}, f32[8,128]{1,0:T(8,128)}) custom-call(f32[512,256]{1,0:T(8,128)S(1)} %get-tuple-element.55.own_ref, bf16[512,256]{1,0:T(8,128)(2,1)S(1)} %collective-permute-done.4.near_ref, bf16[16,8,128]{2,1,0:T(8,128)(2,1)S(1)} %all_to_all.5.bias_ref), custom_call_target="tpu_custom_call" | custom-call | flops 1000 | bytes 4194304 | tf_op jit(solution)/shard_map/pallas_call | solution.py:289
  (3 shorter events, 0.0 us)
Async XLA Ops:
  0.6 11.3 %collective-permute-start = (bf16[512,128]{1,0:T(8,128)(2,1)}, bf16[512,128]{1,0:T(8,128)(2,1)S(1)}, u32[]{:S(2)}, u32[]{:S(2)}) collective-permute-start(bf16[512,128]{1,0:T(8,128)(2,1)} %bitcast.9), channel_id=1, source_target_pairs={{0,8},{8,16},{16,24},{24,32},{32,40},{40,48},{48,56},{56,64},{64,7... | collective-permute-start | bytes 393224 | tf_op jit(solution)/shard_map/ppermute | solution.py:381
  4.5 7.4 %collective-permute-start.1 = (bf16[512,128]{1,0:T(8,128)(2,1)}, bf16[512,128]{1,0:T(8,128)(2,1)S(1)}, u32[]{:S(2)}, u32[]{:S(2)}) collective-permute-start(bf16[512,128]{1,0:T(8,128)(2,1)} %bitcast.11), channel_id=1, source_target_pairs={{0,8},{8,16},{16,24},{24,32},{32,40},{40,48},{48,56},{56,64},{64,7... | collective-permute-start | bytes 393224 | tf_op jit(solution)/shard_map/ppermute | solution.py:381
  8.3 0.7 %copy-start = (s32[1,12]{1,0:T(1,128)S(1)}, s32[1,12]{1,0:T(1,128)}, u32[]{:S(2)}) copy-start(s32[1,12]{1,0:T(1,128)} %len_ref.7) | copy-start | bytes 148
  12.0 8.8 %collective-permute-start.2 = (bf16[512,256]{1,0:T(8,128)(2,1)S(1)}, bf16[512,256]{1,0:T(8,128)(2,1)S(1)}, u32[]{:S(2)}, u32[]{:S(2)}) collective-permute-start(bf16[512,256]{1,0:T(8,128)(2,1)S(1)} %pad_maximum_fusion), channel_id=1, source_target_pairs={{0,8},{8,16},{16,24},{24,32},{32,40},{40,48},{48,56},{56,64},{64,7... | collective-permute-start | bytes 786440 | tf_op jit(solution)/shard_map/ppermute | solution.py:381
  21.6 11.4 %collective-permute-start.3 = (bf16[512,256]{1,0:T(8,128)(2,1)S(1)}, bf16[512,256]{1,0:T(8,128)(2,1)S(1)}, u32[]{:S(2)}, u32[]{:S(2)}) collective-permute-start(bf16[512,256]{1,0:T(8,128)(2,1)S(1)} %get-tuple-element.57), channel_id=1, source_target_pairs={{8,0},{16,8},{24,16},{32,24},{40,32},{48,40},{56,48},{64,56},{72,6... | collective-permute-start | bytes 786440 | tf_op jit(solution)/shard_map/ppermute | solution.py:381
  33.0 1.4 %collective-permute-start.5 = (f32[8,128]{1,0:T(8,128)S(1)}, f32[8,128]{1,0:T(8,128)S(1)}, u32[]{:S(2)}, u32[]{:S(2)}) collective-permute-start(f32[8,128]{1,0:T(8,128)S(1)} %get-tuple-element.60), channel_id=1, source_target_pairs={{0,128},{128,0},{1,129},{129,1},{2,130},{130,2},{3,131},{131,3},{4... | collective-permute-start | bytes 12296 | tf_op jit(solution)/shard_map/ppermute | solution.py:394
  33.1 29.3 %collective-permute-start.4 = (bf16[512,256]{1,0:T(8,128)(2,1)S(1)}, bf16[512,256]{1,0:T(8,128)(2,1)S(1)}, u32[]{:S(2)}, u32[]{:S(2)}) collective-permute-start(bf16[512,256]{1,0:T(8,128)(2,1)S(1)} %add_convert_fusion), channel_id=1, source_target_pairs={{8,0},{16,8},{24,16},{32,24},{40,32},{48,40},{56,48},{64,56},{72,6... | collective-permute-start | bytes 786440 | tf_op jit(solution)/shard_map/ppermute | solution.py:381
where the time goes:
time: 63.5 us; the launch traced here: 63.2 us
  blocking collectives  28 us (44%)
  starting transfers between devices  14.2 us (22%)
  Pallas kernels  12.5 us (20%)
  waiting for transfers between devices  7.06 us (11%)
  between operations  0.77 us (1%)
  local copies, waits for them, and re-layouts  0.65 us (1%)
    all_to_all x1, blocking collectives, body(): lax.all_to_all(jnp.broadcast_to(bias.astype(bf16), (cp, heads, head)), 'c...  28 us
    ppermute x5, starting transfers between devices, shift(): lax.ppermute(x, 'cp', [(i, i + steps) for i in range(max(0, -steps), min(...  14.1 us
    pallas_call x5, Pallas kernels, call(): pl.pallas_call(kernel, out_shape=outs, in_specs=specs, out_specs=out_spec...  12.5 us
    ppermute x5, waiting for transfers between devices, shift(): lax.ppermute(x, 'cp', [(i, i + steps) for i in range(max(0, -steps), min(...  7.06 us
  transfers between devices with their start and end apart: 6, of which 2 were waited for; matrix products, arithmetic and copies ran while one was open for 0% of the time, Pallas kernels for 17%

commit v1 on v0

--- a/solution.py
+++ b/solution.py
@@ -123,6 +123,37 @@
 
 def far_slot(i, tile, first, chunk):
     return pl.ds(pl.multiple_of(i * FAR_CHUNK, FAR_CHUNK), chunk)
+
+
+def plan_far(len_ref, tokens, rows, group, items_ref):
+    ends = doc_ends(len_ref, tokens)
+    span = ROWS // group
+    count, slot = jnp.int32(0), jnp.int32(0)
+    for j in range(rows // ROWS):
+        low0, low1 = low_of(ends, jnp.int32(j * span)), low_of(ends, jnp.int32((j + 1) * span - 1))
+        begin = jnp.maximum(low0 + 2 * tokens, 0) // FAR_CHUNK
+        for last in range(1, tokens // FAR_CHUNK, 2):
+            double = (begin < last).astype(jnp.int32)
+            chunk = last - double
+            masked = (low1 > chunk * FAR_CHUNK - 2 * tokens).astype(jnp.int32)
+            live = (begin <= last).astype(jnp.int32)
+            items_ref[count] = slot * 1024 + double * 512 + j * 64 + chunk * 2 + masked
+            count += live
+            slot += live * (1 + double)
+    return count
+
+
+def each_far(items_ref, count, step):
+    @pl.loop(0, count)
+    def _(i):
+        item = items_ref[i]
+        slot, tile = item // 1024, (item // 64) % 8
+        first = pl.multiple_of((item // 2) % 32 * FAR_CHUNK, FAR_CHUNK)
+        for double in (0, 1):
+
+            @pl.when((item // 512) % 2 == double)
+            def _():
+                step(slot, tile, first, (1 + double) * FAR_CHUNK, item % 2)
 
 
 def hide(x, start, rows, see_ref):
@@ -219,14 +250,22 @@
     dqt_ref[...] = jnp.zeros_like(dqt_ref)
     sum_ref[...] = jnp.zeros_like(sum_ref)
     kt_ref[...] = k_ref[...].T
-    count = plan(len_ref, tokens, q_ref.shape[0], group, origin, FAR_CHUNK, items_ref)
-    each_item(items_ref, 0, count, FAR_CHUNK, functools.partial(
-        add_stats, scale2, origin, FAR_CHUNK, q_ref, g_ref, k_ref, v_ref, see_ref, run_ref, s_ref, dp_ref, far_slot))
+    count = plan_far(len_ref, tokens, q_ref.shape[0], group, items_ref)
+
+    def add(slot, tile, first, chunk, masked):
+        for hidden in (0, 1):
+
+            @pl.when(masked == hidden)
+            def _():
+                add_stats(scale2, origin, chunk, q_ref, g_ref, k_ref, v_ref, see_ref, run_ref, s_ref, dp_ref, far_slot,
+                          slot, tile, first, hidden == 1)
+
+    each_far(items_ref, count, add)
     total = run_ref[1:2, :]
     st_ref[0:1, :] = run_ref[0:1, :] + jnp.log2(total)
     st_ref[1:2, :] = run_ref[2:3, :] / total
-    each_kept(items_ref, 0, count, FAR_CHUNK, functools.partial(
-        add_grads, FAR_CHUNK, q_ref, g_ref, kt_ref, st_ref, dqt_ref, sum_ref, s_ref, dp_ref, far_slot))
+    each_far(items_ref, count, lambda slot, tile, first, chunk, masked: add_grads(
+        chunk, q_ref, g_ref, kt_ref, st_ref, dqt_ref, sum_ref, s_ref, dp_ref, far_slot, slot, tile, first))
     far_ref[...] = sum_ref[...].astype(far_ref.dtype)
 
 

time: 63.5 us -> 61.8 us (0.973); the launches traced: 63.2 us -> 60.8 us
  blocking collectives: 28 us -> 25.4 us
    all_to_all x1, blocking collectives: 28 us -> 25.4 us  [body(): lax.all_to_all(jnp.broadcast_to(bias.astype(bf16), (cp, heads, head)), 'c...]
  transfers between devices with their start and end apart: 6 -> 6, of which waited for: 2 -> 2; matrix products, arithmetic and copies ran while one was open for 0% -> 0% of each run, Pallas kernels for 17% -> 18%
where the time goes in v1:
time: 61.8 us; the launch traced here: 60.8 us
  blocking collectives  25.4 us (41%)
  starting transfers between devices  14.2 us (23%)
  Pallas kernels  12.4 us (20%)
  waiting for transfers between devices  7.25 us (12%)
  between operations  0.77 us (1%)
  local copies, waits for them, and re-layouts  0.65 us (1%)
    all_to_all x1, blocking collectives, body(): lax.all_to_all(jnp.broadcast_to(bias.astype(bf16), (cp, heads, head)), 'c...  25.4 us
    ppermute x5, starting transfers between devices, shift(): lax.ppermute(x, 'cp', [(i, i + steps) for i in range(max(0, -steps), min(...  14.1 us
    pallas_call x5, Pallas kernels, call(): pl.pallas_call(kernel, out_shape=outs, in_specs=specs, out_specs=out_spec...  12.4 us
    ppermute x5, waiting for transfers between devices, shift(): lax.ppermute(x, 'cp', [(i, i + steps) for i in range(max(0, -steps), min(...  7.24 us
  transfers between devices with their start and end apart: 6, of which 2 were waited for; matrix products, arithmetic and copies ran while one was open for 0% of the time, Pallas kernels for 18%

profile of v1, /device:TPU:2, one launch (start us, length us, event | category | flops | bytes accessed | tf_op | source)
XLA Modules:
  0.0 60.8 jit_solution(16229959049479035187)
XLA Ops:
  0.6 3.8 %collective-permute-start = (bf16[512,128]{1,0:T(8,128)(2,1)}, bf16[512,128]{1,0:T(8,128)(2,1)S(1)}, u32[]{:S(2)}, u32[]{:S(2)}) collective-permute-start(bf16[512,128]{1,0:T(8,128)(2,1)} %bitcast.9), channel_id=1, source_target_pairs={{0,8},{8,16},{16,24},{24,32},{32,40},{40,48},{48,56},{56,64},{64,7... | collective-permute-start | bytes 393224 | tf_op jit(solution)/shard_map/ppermute | solution.py:420
  4.5 3.8 %collective-permute-start.1 = (bf16[512,128]{1,0:T(8,128)(2,1)}, bf16[512,128]{1,0:T(8,128)(2,1)S(1)}, u32[]{:S(2)}, u32[]{:S(2)}) collective-permute-start(bf16[512,128]{1,0:T(8,128)(2,1)} %bitcast.11), channel_id=1, source_target_pairs={{0,8},{8,16},{16,24},{24,32},{32,40},{40,48},{48,56},{56,64},{64,7... | collective-permute-start | bytes 393224 | tf_op jit(solution)/shard_map/ppermute | solution.py:420
  8.3 0.0 copy-start
  8.3 0.6 %copy-done = s32[1,12]{1,0:T(1,128)S(1)} copy-done((s32[1,12]{1,0:T(1,128)S(1)}, s32[1,12]{1,0:T(1,128)}, u32[]{:S(2)}) %copy-start) | copy-done | bytes 72
  9.0 2.9 %shard_map.84 = (bf16[4096,128]{1,0:T(8,128)(2,1)S(1)}, bf16[4096,128]{1,0:T(8,128)(2,1)S(1)}, bf16[512,128]{1,0:T(8,128)(2,1)S(1)}, bf16[512,128]{1,0:T(8,128)(...) custom-call(s32[1,12]{1,0:T(1,128)S(1)} %copy-done, ...), custom_call_target="tpu_custom_call" | custom-call | flops 536870912 | bytes 4194304 | tf_op jit(solution)/shard_map/pallas_call | solution.py:328
  11.9 0.0 collective-permute-done.k1_ref
  11.9 0.0 collective-permute-done.1.v1_ref
  12.0 3.8 %collective-permute-start.2 = (bf16[512,256]{1,0:T(8,128)(2,1)S(1)}, bf16[512,256]{1,0:T(8,128)(2,1)S(1)}, u32[]{:S(2)}, u32[]{:S(2)}) collective-permute-start(bf16[512,256]{1,0:T(8,128)(2,1)S(1)} %pad_maximum_fusion), channel_id=1, source_target_pairs={{0,8},{8,16},{16,24},{24,32},{32,40},{40,48},{48,56},{56,64},{64,7... | collective-permute-start | bytes 786440 | tf_op jit(solution)/shard_map/ppermute | solution.py:420
  15.8 2.7 %shard_map.85 = (f32[3,4096]{1,0:T(4,128)S(1)}, f32[512,2048]{1,0:T(8,128)S(1)}, f32[512,2048]{1,0:T(8,128)S(1)}, f32[1024,2048]{1,0:T(8,128)S(1)}, f32[1024,204...) custom-call(s32[1,12]{1,0:T(1,128)S(1)} %copy-done, ...), custom_call_target="tpu_custom_call" | custom-call | flops 1610612736 | bytes 4194304 | tf_op jit(solution)/shard_map/pallas_call | solution.py:328
  18.5 2.2 %collective-permute-done.2.kv_ref = bf16[512,256]{1,0:T(8,128)(2,1)S(1)} collective-permute-done((bf16[512,256]{1,0:T(8,128)(2,1)S(1)}, bf16[512,256]{1,0:T(8,128)(2,1)S(1)}, u32[]{:S(2)}, u32[]{:S(2)}) %collective-permute-start.2) | collective-permute-done | bytes 262176 | tf_op jit(solution)/shard_map/ppermute | solution.py:420
  20.8 0.9 %shard_map.86 = (f32[2,4096]{1,0:T(2,128)S(1)}, bf16[512,256]{1,0:T(8,128)(2,1)S(1)}, f32[128,4096]{1,0:T(8,128)S(1)}) custom-call(s32[1,12]{1,0:T(1,128)S(1)} %copy-done, bf16[4096,128]{1,0:T(8,128)(2,1)S(1)} %get-tuple-element.34.q_ref, bf16[4096,128]{1,0:T(8,128)(2,1)S(1)} %get-tuple-element.35.g_ref, bf16[512,256]{1,0:T(8,128)(2,1)S(1)} %collective-permute-done.2.kv_ref, ...), custom_call_target="tpu_custom_call" | custom-call | flops 536870912 | bytes 4194304 | tf_op jit(solution)/shard_map/pallas_call | solution.py:328
  21.7 1.3 %collective-permute-start.3 = (bf16[512,256]{1,0:T(8,128)(2,1)S(1)}, bf16[512,256]{1,0:T(8,128)(2,1)S(1)}, u32[]{:S(2)}, u32[]{:S(2)}) collective-permute-start(bf16[512,256]{1,0:T(8,128)(2,1)S(1)} %get-tuple-element.57), channel_id=1, source_target_pairs={{8,0},{16,8},{24,16},{32,24},{40,32},{48,40},{56,48},{64,56},{72,6... | collective-permute-start | bytes 786440 | tf_op jit(solution)/shard_map/ppermute | solution.py:420
  23.0 5.1 %shard_map.87 = (bf16[4096,128]{1,0:T(8,128)(2,1)}, f32[512,256]{1,0:T(8,128)S(1)}, f32[512,256]{1,0:T(8,128)S(1)}, f32[8,128]{1,0:T(8,128)S(1)}, f32[128,4096]{1,0:T(8,128)S(1)}) custom-call(s32[1,12]{1,0:T(1,128)S(1)} %copy-done, bf16[4096,128]{1,0:T(8,128)(2,1)S(1)} %get-tuple-element.34.q_ref, ...), custom_call_target="tpu_custom_call", output_to_operand_aliasing={{4}: (12, {})} | custom-call | flops 3221225472 | bytes 4194304 | tf_op jit(solution)/shard_map/pallas_call | solution.py:328
  28.1 5.0 %collective-permute-done.3 = bf16[512,256]{1,0:T(8,128)(2,1)S(1)} collective-permute-done((bf16[512,256]{1,0:T(8,128)(2,1)S(1)}, bf16[512,256]{1,0:T(8,128)(2,1)S(1)}, u32[]{:S(2)}, u32[]{:S(2)}) %collective-permute-start.3) | collective-permute-done | bytes 262176 | tf_op jit(solution)/shard_map/ppermute | solution.py:420
  33.1 0.1 add_convert_fusion
  33.2 0.1 collective-permute-start.5
  33.3 1.3 %collective-permute-start.4 = (bf16[512,256]{1,0:T(8,128)(2,1)S(1)}, bf16[512,256]{1,0:T(8,128)(2,1)S(1)}, u32[]{:S(2)}, u32[]{:S(2)}) collective-permute-start(bf16[512,256]{1,0:T(8,128)(2,1)S(1)} %add_convert_fusion), channel_id=1, source_target_pairs={{8,0},{16,8},{24,16},{32,24},{40,32},{48,40},{56,48},{64,56},{72,6... | collective-permute-start | bytes 786440 | tf_op jit(solution)/shard_map/ppermute | solution.py:420
  34.6 0.0 collective-permute-done.5
  34.6 25.4 %all_to_all.5.bias_ref = bf16[16,8,128]{2,1,0:T(8,128)(2,1)S(1)} all-to-all(bf16[16,8,128]{2,1,0:T(8,128)(2,1)S(1)} %broadcast_in_dim.3), channel_id=1, replica_groups=mesh['dp'=2,'cp'=16,'tp'=8] {'cp'}, dimensions={0} | all-to-all | bytes 65536 | tf_op jit(solution)/shard_map/all_to_all | solution.py:434
  60.0 0.0 collective-permute-done.4.near_ref
  60.0 0.8 %shard_map.88 = (bf16[512,128]{1,0:T(8,128)(2,1)}, bf16[512,128]{1,0:T(8,128)(2,1)}, f32[8,128]{1,0:T(8,128)}) custom-call(f32[512,256]{1,0:T(8,128)S(1)} %get-tuple-element.55.own_ref, bf16[512,256]{1,0:T(8,128)(2,1)S(1)} %collective-permute-done.4.near_ref, bf16[16,8,128]{2,1,0:T(8,128)(2,1)S(1)} %all_to_all.5.bias_ref), custom_call_target="tpu_custom_call" | custom-call | flops 1000 | bytes 4194304 | tf_op jit(solution)/shard_map/pallas_call | solution.py:328
  (3 shorter events, 0.0 us)
Async XLA Ops:
  0.6 11.3 %collective-permute-start = (bf16[512,128]{1,0:T(8,128)(2,1)}, bf16[512,128]{1,0:T(8,128)(2,1)S(1)}, u32[]{:S(2)}, u32[]{:S(2)}) collective-permute-start(bf16[512,128]{1,0:T(8,128)(2,1)} %bitcast.9), channel_id=1, source_target_pairs={{0,8},{8,16},{16,24},{24,32},{32,40},{40,48},{48,56},{56,64},{64,7... | collective-permute-start | bytes 393224 | tf_op jit(solution)/shard_map/ppermute | solution.py:420
  4.5 7.4 %collective-permute-start.1 = (bf16[512,128]{1,0:T(8,128)(2,1)}, bf16[512,128]{1,0:T(8,128)(2,1)S(1)}, u32[]{:S(2)}, u32[]{:S(2)}) collective-permute-start(bf16[512,128]{1,0:T(8,128)(2,1)} %bitcast.11), channel_id=1, source_target_pairs={{0,8},{8,16},{16,24},{24,32},{32,40},{40,48},{48,56},{56,64},{64,7... | collective-permute-start | bytes 393224 | tf_op jit(solution)/shard_map/ppermute | solution.py:420
  8.3 0.7 %copy-start = (s32[1,12]{1,0:T(1,128)S(1)}, s32[1,12]{1,0:T(1,128)}, u32[]{:S(2)}) copy-start(s32[1,12]{1,0:T(1,128)} %len_ref.7) | copy-start | bytes 148
  12.0 8.8 %collective-permute-start.2 = (bf16[512,256]{1,0:T(8,128)(2,1)S(1)}, bf16[512,256]{1,0:T(8,128)(2,1)S(1)}, u32[]{:S(2)}, u32[]{:S(2)}) collective-permute-start(bf16[512,256]{1,0:T(8,128)(2,1)S(1)} %pad_maximum_fusion), channel_id=1, source_target_pairs={{0,8},{8,16},{16,24},{24,32},{32,40},{40,48},{48,56},{56,64},{64,7... | collective-permute-start | bytes 786440 | tf_op jit(solution)/shard_map/ppermute | solution.py:420
  21.7 11.4 %collective-permute-start.3 = (bf16[512,256]{1,0:T(8,128)(2,1)S(1)}, bf16[512,256]{1,0:T(8,128)(2,1)S(1)}, u32[]{:S(2)}, u32[]{:S(2)}) collective-permute-start(bf16[512,256]{1,0:T(8,128)(2,1)S(1)} %get-tuple-element.57), channel_id=1, source_target_pairs={{8,0},{16,8},{24,16},{32,24},{40,32},{48,40},{56,48},{64,56},{72,6... | collective-permute-start | bytes 786440 | tf_op jit(solution)/shard_map/ppermute | solution.py:420
  33.2 1.4 %collective-permute-start.5 = (f32[8,128]{1,0:T(8,128)S(1)}, f32[8,128]{1,0:T(8,128)S(1)}, u32[]{:S(2)}, u32[]{:S(2)}) collective-permute-start(f32[8,128]{1,0:T(8,128)S(1)} %get-tuple-element.60), channel_id=1, source_target_pairs={{0,128},{128,0},{1,129},{129,1},{2,130},{130,2},{3,131},{131,3},{4... | collective-permute-start | bytes 12296 | tf_op jit(solution)/shard_map/ppermute | solution.py:433
  33.3 26.8 %collective-permute-start.4 = (bf16[512,256]{1,0:T(8,128)(2,1)S(1)}, bf16[512,256]{1,0:T(8,128)(2,1)S(1)}, u32[]{:S(2)}, u32[]{:S(2)}) collective-permute-start(bf16[512,256]{1,0:T(8,128)(2,1)S(1)} %add_convert_fusion), channel_id=1, source_target_pairs={{8,0},{16,8},{24,16},{32,24},{40,32},{48,40},{56,48},{64,56},{72,6... | collective-permute-start | bytes 786440 | tf_op jit(solution)/shard_map/ppermute | solution.py:420
